TPU v7x, 32 devices: a whole 2x2x4 slice. The times are simulated.
32 devices in a mesh: dp: 8 (over y, x, core), tensor: 4 (over z).
Axes of the slice: x: 2, y: 2, z: 4, core: 2. Of those that a mesh axis runs over, the one named last changes fastest.
Arguments:
- layer_input_rows: bfloat16 [512, 32, 768], P('tensor', 'dp'), may hold values from -6 to 6
- sentence_index_row: int32 [32, 512], P('dp'), may hold values from 0 to 7, as said below
- padding_mask: int32 [32, 512], P('dp'), may hold values from 0 to 1, as said below
- output_gradient: bfloat16 [512, 32, 768], P('tensor', 'dp'), may hold values from -6 to 6
- owner_rank: int32 [769], replicated, may hold values from 0 to 7, as said below
- master_state: float32 [4, 1536, 2304], P('tensor', 'dp'), may hold values from -1.5 to 1.5
- first_moment: float32 [4, 1536, 2304], P('tensor', 'dp')
- second_moment: float32 [4, 1536, 2304], P('tensor', 'dp'), as said below
Outputs:
- layer_out: float32 [512, 32, 768], P('tensor', 'dp')
- pooled_mean: float32 [32, 8, 768], P('dp', None, 'tensor')
- input_grad: float32 [512, 32, 768], P('tensor', 'dp')
- new_master: float32 [4, 1536, 2304], P('tensor', 'dp')
- new_first: float32 [4, 1536, 2304], P('tensor', 'dp')
- new_second: float32 [4, 1536, 2304], P('tensor', 'dp')
- norm_grads: float32 [6, 768], P(None, 'tensor')
Inputs may be any that keep to these rules, and one draw needn't show every extreme that they name: `owner_rank`: each dp index owns at most 192 blocks, and one of them owns exactly 192. `sentence_index_row`: ids never fall along a row; padding positions carry id 8 - 1 = 7. `padding_mask`: in every row the ones come first and cover at least 320 positions. `second_moment`: positive.
All inputs are finite; a program needn't handle non-finite values.
Results may differ from a plain program's by a relative error of at most 0.017.
Values may be sent and summed in bfloat16 or wider, within the bound.
A program may use at most 192 MiB of HBM per device.

v0:
```python
import jax
import numpy as np
import jax.numpy as jnp
from jax import lax
from jax.experimental import pallas as pl
from jax.experimental.pallas import tpu as pltpu
from jax.sharding import PartitionSpec as P

MODEL_WIDTH = 768
HEAD_DIM = 64
FF = 3072
SMAX = 8
STEP = 10


NORM_EPS = 1e-05
ADAM_EPS = 1e-08
BETA_ONE = 0.9
BETA_TWO = 0.999
DECAY_RATE = 0.01
MASKED = -1e30
exact_precision = lax.Precision.HIGHEST


def slot_tables(owner_rank, per_owner):
    ordinal = jnp.arange(owner_rank.shape[0], dtype=jnp.int32)
    same_owner = owner_rank[:, None] == owner_rank[None, :]
    earlier = ordinal[None, :] < ordinal[:, None]
    ranking = jnp.sum((same_owner & earlier).astype(jnp.int32), axis=1)
    return owner_rank * per_owner + ranking


def slot_blocks(slot_of, wanted):
    matches = slot_of[None, :] == wanted[:, None]
    filled = jnp.any(matches, axis=1)
    ordinal = jnp.arange(slot_of.shape[0], dtype=jnp.int32)
    block_of = jnp.sum(jnp.where(matches, ordinal[None, :], 0), axis=1)
    return (block_of, filled)


def step_rates(token_position, width, hidden, tensor_size):
    width_loc = width // tensor_size
    ffn_loc = hidden // tensor_size
    end_up = width * ffn_loc
    end_down = end_up + ffn_loc * width
    end_qkv = end_down + width * 3 * width_loc
    end_out = end_qkv + width_loc * width
    offset = token_position - end_out
    first_gain = (offset >= 4 * width_loc + ffn_loc) & (offset < 5 * width_loc + ffn_loc)
    second_gain = (offset >= 6 * width_loc + ffn_loc) & (offset < 7 * width_loc + ffn_loc)
    small_rate = jnp.where(first_gain | second_gain, 0.2, 0.1)
    step_rate = jnp.where(
        token_position < end_up,
        width ** (-0.5),
        jnp.where(
            token_position < end_down,
            hidden ** (-0.5),
            jnp.where(
                token_position < end_qkv,
                width ** (-0.5),
                jnp.where(token_position < end_out, 4.0 * width ** (-0.5), small_rate),
            ),
        ),
    )
    decay_on = (token_position < end_out).astype(jnp.float32)
    return (step_rate.astype(jnp.float32), decay_on)


def adamw(gradient, moment, square, weight, step_rate, decay_on, filled):
    new_moment = BETA_ONE * moment + (1.0 - BETA_ONE) * gradient
    new_square = BETA_TWO * square + (1.0 - BETA_TWO) * gradient * gradient
    unbiased = new_moment / (1.0 - BETA_ONE**STEP)
    divisor = jnp.sqrt(new_square / (1.0 - BETA_TWO**STEP)) + ADAM_EPS
    new_weight = weight - step_rate * (unbiased / divisor + DECAY_RATE * decay_on * weight)
    zeroed = jnp.zeros_like(weight)
    return (
        jnp.where(filled, new_weight, zeroed),
        jnp.where(filled, new_moment, zeroed),
        jnp.where(filled, new_square, zeroed),
    )


def normalize(values):
    centred = values - jnp.mean(values, axis=-1, keepdims=True)
    inv_dev = lax.rsqrt(jnp.mean(centred * centred, axis=-1, keepdims=True) + NORM_EPS)
    return (centred * inv_dev, inv_dev)


def norm_back(grad_scaled, normed, inv_dev):
    first_mean = jnp.mean(grad_scaled, axis=-1, keepdims=True)
    second_mean = jnp.mean(grad_scaled * normed, axis=-1, keepdims=True)
    return inv_dev * (grad_scaled - first_mean - normed * second_mean)


def allowed_pairs(sentence_labels, real_token_flags):
    row_len = sentence_labels.shape[-1]
    same_sent = sentence_labels[:, :, None] == sentence_labels[:, None, :]
    live = (real_token_flags[:, :, None] == 1) & (real_token_flags[:, None, :] == 1)
    diagonal = jnp.eye(row_len, dtype=bool)[None]
    return same_sent & live | diagonal


def masked_scores(queries, key_rows, allowed, scaling):
    scores = (
        jnp.einsum("qshe,kshe->shqk", queries, key_rows, preferred_element_type=jnp.float32)
        * scaling
    )
    return jnp.where(allowed[:, None], scores, MASKED)


def split_flat(flat_all, width_loc, ffn_loc):
    end_up = MODEL_WIDTH * ffn_loc
    end_down = end_up + ffn_loc * MODEL_WIDTH
    end_qkv = end_down + MODEL_WIDTH * 3 * width_loc
    end_out = end_qkv + width_loc * MODEL_WIDTH
    return (
        flat_all[:end_up].reshape(MODEL_WIDTH, ffn_loc),
        flat_all[end_up:end_down].reshape(ffn_loc, MODEL_WIDTH),
        flat_all[end_down:end_qkv].reshape(MODEL_WIDTH, 3 * width_loc),
        flat_all[end_qkv:end_out].reshape(width_loc, MODEL_WIDTH),
        flat_all[end_out:],
    )


def local_general(
    layer_input_rows,
    sentence_index_row,
    padding_mask,
    output_gradient,
    owner_rank,
    master_state,
    first_moment,
    second_moment,
):
    tensor_size = lax.axis_size("tensor")
    tensor_at = lax.axis_index("tensor")
    data_size = lax.axis_size("dp")
    data_at = lax.axis_index("dp")
    width_loc = MODEL_WIDTH // tensor_size
    ffn_loc = FF // tensor_size
    heads_loc = width_loc // HEAD_DIM
    quarter = layer_input_rows.shape[0]
    seq_count = layer_input_rows.shape[1]
    row_len = quarter * tensor_size
    per_owner = master_state.shape[1]
    block_len = master_state.shape[2]
    nblocks = owner_rank.shape[0]
    slot_of = slot_tables(owner_rank, per_owner)
    gathered = lax.all_gather(master_state.astype(jnp.bfloat16), "dp", axis=1, tiled=True)[0]
    flat_weights = gathered[slot_of].reshape(nblocks * block_len)
    up_weight, down_weight, w_qkv, w_out, small_part = split_flat(flat_weights, width_loc, ffn_loc)
    bias_q = small_part[:width_loc].astype(jnp.float32)
    bias_v = small_part[width_loc : 2 * width_loc].astype(jnp.float32)
    expand_bias = small_part[2 * width_loc : 2 * width_loc + ffn_loc].astype(jnp.float32)
    norm_parts = small_part[2 * width_loc + ffn_loc :].reshape(6, width_loc)
    full_rows, norm_whole = (
        lax.all_gather(layer_input_rows, "tensor", axis=0, tiled=True),
        lax.all_gather(norm_parts, "tensor", axis=1, tiled=True),
    )
    norm_all = norm_whole.astype(jnp.float32)
    bias_out, bias_down = (norm_all[0], norm_all[1])
    gain_one, shift_one, gain_two, shift_two = (norm_all[2], norm_all[3], norm_all[4], norm_all[5])
    qkv_lin = jnp.einsum("lsd,de->lse", full_rows, w_qkv, preferred_element_type=jnp.float32)
    bias_qkv = jnp.concatenate([bias_q, jnp.zeros((width_loc,), jnp.float32), bias_v])
    qkv = (qkv_lin + bias_qkv).astype(jnp.bfloat16)
    queries = qkv[:, :, :width_loc].reshape(row_len, seq_count, heads_loc, HEAD_DIM)
    key_rows = qkv[:, :, width_loc : 2 * width_loc].reshape(row_len, seq_count, heads_loc, HEAD_DIM)
    values = qkv[:, :, 2 * width_loc :].reshape(row_len, seq_count, heads_loc, HEAD_DIM)
    scaling = HEAD_DIM ** (-0.5)
    allowed = allowed_pairs(sentence_index_row, padding_mask)
    scores = masked_scores(queries, key_rows, allowed, scaling)
    row_peak = jnp.max(scores, axis=-1, keepdims=True)
    log_total = row_peak + jnp.log(jnp.sum(jnp.exp(scores - row_peak), axis=-1, keepdims=True))
    prob_low = jnp.exp(scores - log_total).astype(jnp.bfloat16)
    attended = jnp.einsum("shqk,kshe->qshe", prob_low, values, preferred_element_type=jnp.float32)
    attended = attended.astype(jnp.bfloat16).reshape(row_len, seq_count, width_loc)
    portion_rows = attended
    attn_rows = lax.psum_scatter(
        jnp.einsum("lse,ed->lsd", portion_rows, w_out, preferred_element_type=jnp.float32).astype(
            jnp.bfloat16
        ),
        "tensor",
        scatter_dimension=0,
        tiled=True,
    ).astype(jnp.float32)
    z_one = layer_input_rows.astype(jnp.float32) + attn_rows + bias_out
    normed_one, inv_one = normalize(z_one)
    h_mine = normed_one * gain_one + shift_one
    hidden_narrow_whole = lax.all_gather(h_mine.astype(jnp.bfloat16), "tensor", axis=0, tiled=True)
    up_pre = (
        jnp.einsum(
            "wer,rb->web", hidden_narrow_whole, up_weight, preferred_element_type=jnp.float32
        )
        + expand_bias
    )
    activation_narrow = jax.nn.gelu(up_pre, approximate=False).astype(jnp.bfloat16)
    portion_rows = activation_narrow
    down_rows = lax.psum_scatter(
        jnp.einsum(
            "aij,jb->aib", portion_rows, down_weight, preferred_element_type=jnp.float32
        ).astype(jnp.bfloat16),
        "tensor",
        scatter_dimension=0,
        tiled=True,
    ).astype(jnp.float32)
    z_two = h_mine + down_rows + bias_down
    normed_two, inv_two = normalize(z_two)
    layer_out = normed_two * gain_two + shift_two
    seg_mine = lax.dynamic_slice_in_dim(sentence_index_row, tensor_at * quarter, quarter, 1)
    valid_mine = lax.dynamic_slice_in_dim(padding_mask, tensor_at * quarter, quarter, 1)
    sent_ids = jnp.arange(SMAX, dtype=jnp.int32)
    onehot_mine = (
        (seg_mine[:, :, None] == sent_ids[None, None, :]) & (valid_mine[:, :, None] == 1)
    ).astype(jnp.float32)
    pool_part = jnp.einsum("slc,lsd->scd", onehot_mine, layer_out, precision=exact_precision)
    onehot_full = (
        (sentence_index_row[:, :, None] == sent_ids[None, None, :])
        & (padding_mask[:, :, None] == 1)
    ).astype(jnp.float32)
    counts = jnp.sum(onehot_full, axis=1)
    grad_out = output_gradient.astype(jnp.float32) * valid_mine.T[:, :, None].astype(jnp.float32)
    d_gain_two = jnp.sum(grad_out * normed_two, axis=(0, 1))
    d_shift_two = jnp.sum(grad_out, axis=(0, 1))
    dz_two = norm_back(grad_out * gain_two, normed_two, inv_two)
    d_bias_down = jnp.sum(dz_two, axis=(0, 1))
    second_sum_gradient_wide = lax.all_gather(
        dz_two.astype(jnp.bfloat16), "tensor", axis=0, tiled=True
    )
    down_weight_gradient = jnp.einsum(
        "ipo,ipr->or",
        activation_narrow,
        second_sum_gradient_wide,
        preferred_element_type=jnp.float32,
    )
    activation_gradient = jnp.einsum(
        "ugp,jp->ugj", second_sum_gradient_wide, down_weight, preferred_element_type=jnp.float32
    )
    gelu_pull = jax.vjp(lambda pre_act: jax.nn.gelu(pre_act, approximate=False), up_pre)[1]
    d_up = gelu_pull(activation_gradient)[0]
    d_bias_up = jnp.sum(d_up, axis=(0, 1))
    expand_gradient_narrow = d_up.astype(jnp.bfloat16)
    up_weight_gradient = jnp.einsum(
        "iux,iuy->xy",
        hidden_narrow_whole,
        expand_gradient_narrow,
        preferred_element_type=jnp.float32,
    )
    portion_rows = expand_gradient_narrow
    dh_rows = lax.psum_scatter(
        jnp.einsum(
            "uih,vh->uiv", portion_rows, up_weight, preferred_element_type=jnp.float32
        ).astype(jnp.bfloat16),
        "tensor",
        scatter_dimension=0,
        tiled=True,
    ).astype(jnp.float32)
    dh_mine = dz_two + dh_rows
    d_gain_one = jnp.sum(dh_mine * normed_one, axis=(0, 1))
    d_shift_one = jnp.sum(dh_mine, axis=(0, 1))
    dz_one = norm_back(dh_mine * gain_one, normed_one, inv_one)
    d_bias_out = jnp.sum(dz_one, axis=(0, 1))
    dz_one_full = lax.all_gather(dz_one.astype(jnp.bfloat16), "tensor", axis=0, tiled=True)
    d_w_out = jnp.einsum("lse,lsd->ed", attended, dz_one_full, preferred_element_type=jnp.float32)
    d_attended = jnp.einsum("lsd,ed->lse", dz_one_full, w_out, preferred_element_type=jnp.float32)
    d_attended = d_attended.astype(jnp.bfloat16).reshape(row_len, seq_count, heads_loc, HEAD_DIM)
    scores_again = masked_scores(queries, key_rows, allowed, scaling)
    attn_prob = jnp.exp(scores_again - log_total)
    prob_again = attn_prob.astype(jnp.bfloat16)
    d_prob = jnp.einsum("qshe,kshe->shqk", d_attended, values, preferred_element_type=jnp.float32)
    d_values = jnp.einsum(
        "shqk,qshe->kshe", prob_again, d_attended, preferred_element_type=jnp.float32
    )
    inner = jnp.sum(d_prob * attn_prob, axis=-1, keepdims=True)
    d_scores = (attn_prob * (d_prob - inner)).astype(jnp.bfloat16)
    d_queries = (
        jnp.einsum("shqk,kshe->qshe", d_scores, key_rows, preferred_element_type=jnp.float32)
        * scaling
    )
    d_keys = (
        jnp.einsum("shqk,qshe->kshe", d_scores, queries, preferred_element_type=jnp.float32)
        * scaling
    )
    d_bias_q = jnp.sum(d_queries, axis=(0, 1)).reshape(width_loc)
    d_bias_v = jnp.sum(d_values, axis=(0, 1)).reshape(width_loc)
    d_qkv_low = jnp.concatenate(
        [
            d_queries.reshape(row_len, seq_count, width_loc),
            d_keys.reshape(row_len, seq_count, width_loc),
            d_values.reshape(row_len, seq_count, width_loc),
        ],
        axis=2,
    ).astype(jnp.bfloat16)
    d_w_qkv = jnp.einsum("lsd,lse->de", full_rows, d_qkv_low, preferred_element_type=jnp.float32)
    portion_rows = d_qkv_low
    dx_rows = lax.psum_scatter(
        jnp.einsum("lse,de->lsd", portion_rows, w_qkv, preferred_element_type=jnp.float32).astype(
            jnp.bfloat16
        ),
        "tensor",
        scatter_dimension=0,
        tiled=True,
    ).astype(jnp.float32)
    input_grad = dz_one + dx_rows
    shared_grads = jnp.stack(
        [d_bias_out, d_bias_down, d_gain_one, d_shift_one, d_gain_two, d_shift_two]
    )[None]
    pool_sum, shared_sum = (
        lax.psum_scatter(
            pool_part.astype(jnp.bfloat16), "tensor", scatter_dimension=2, tiled=True
        ).astype(jnp.float32),
        lax.psum_scatter(
            shared_grads.astype(jnp.bfloat16), "tensor", scatter_dimension=2, tiled=True
        ).astype(jnp.float32),
    )
    pooled_mean = pool_sum / jnp.maximum(counts, 1.0)[:, :, None]
    flat_grads = jnp.concatenate(
        [
            up_weight_gradient.reshape(-1),
            down_weight_gradient.reshape(-1),
            d_w_qkv.reshape(-1),
            d_w_out.reshape(-1),
            d_bias_q,
            d_bias_v,
            d_bias_up,
            shared_sum.reshape(-1),
        ]
    )
    grad_blocks = flat_grads.reshape(nblocks, block_len)
    wanted = data_at * per_owner + jnp.arange(per_owner, dtype=jnp.int32)
    block_of, filled = slot_blocks(slot_of, wanted)
    slot_grads = (
        jnp.zeros((data_size * per_owner, block_len), jnp.float32).at[slot_of].set(grad_blocks)
    )
    owned_grads = lax.psum_scatter(slot_grads, "dp", scatter_dimension=0, tiled=True)
    norm_grads = lax.psum(shared_sum[0], "dp")
    token_position = block_of[:, None] * block_len + jnp.arange(block_len, dtype=jnp.int32)[None, :]
    step_rate, decay_on = step_rates(token_position, MODEL_WIDTH, FF, tensor_size)
    new_master, new_first, new_second = adamw(
        owned_grads,
        first_moment[0],
        second_moment[0],
        master_state[0],
        step_rate,
        decay_on,
        filled[:, None],
    )
    return (
        layer_out,
        pooled_mean,
        input_grad,
        new_master[None],
        new_first[None],
        new_second[None],
        norm_grads,
    )


MESH = pl.DeviceIdType.MESH
BF = jnp.bfloat16
F32 = jnp.float32
WEIGHTS = ((768, 96), (768, 96), (768, 96))
MIB = 2**20


class Place:
    def __init__(self):
        d = lax.axis_index("dp")
        self.t = lax.axis_index("tensor")
        self.c = d % 2
        self.x = (d // 2) % 2
        self.y = d // 4
        self.xy = d // 2
        self.core = (d + 1 - 2 * self.c, self.t)
        self.right = (d + 2 - 4 * self.x, self.t)
        self.down = (d + 4 - 8 * self.y, self.t)
        self.diag = (d + 6 - 4 * self.x - 8 * self.y, self.t)
        self.deep = [None] + [(d, (self.t + k) % 4) for k in (1, 2, 3)]
        self.ahead = [(self.t + k) % 4 for k in range(4)]
        self.behind = [(self.t + 4 - k) % 4 for k in range(4)]

    def hail(self):
        peers = [self.core, self.right, self.down, self.diag] + self.deep[1:]
        for peer in peers:
            pl.semaphore_signal(
                pltpu.get_barrier_semaphore(), inc=1, device_id=peer, device_id_type=MESH
            )

    def meet(self):
        pl.semaphore_wait(pltpu.get_barrier_semaphore(), 7)


class Sender:
    def __init__(self, send_sems, recv_sems, local_sems):
        self.sems = (send_sems, recv_sems, local_sems)
        self.used = 0
        self.used_local = 0
        self.open = []

    def send(self, src, dst, peer):
        i = self.used
        self.used += 1
        copy = pltpu.make_async_remote_copy(
            src_ref=src,
            dst_ref=dst,
            send_sem=self.sems[0].at[i],
            recv_sem=self.sems[1].at[i],
            device_id=peer,
            device_id_type=MESH,
        )
        copy.start()
        self.open.append(copy)
        return copy

    def copy(self, src, dst):
        i = self.used_local
        self.used_local += 1
        copy = pltpu.make_async_copy(src, dst, self.sems[2].at[i])
        copy.start()
        return copy

    def sent(self, copy):
        copy.wait_send()
        self.open = [other for other in self.open if other is not copy]

    def finish(self):
        for copy in self.open:
            copy.wait_send()


def rows_of(place, rows, at=None):
    at = place.xy if at is None else at
    return pl.ds(pl.multiple_of(place.c * (4 * rows) + at * rows, 32), rows)


def half_of(place, rows):
    return pl.ds(pl.multiple_of(place.c * (4 * rows), 128), 4 * rows)


def interleave(size, parts):
    group = size // parts
    out_row = lax.broadcasted_iota(jnp.int32, (size, size), 0)
    col = lax.broadcasted_iota(jnp.int32, (size, size), 1)
    part = jnp.zeros((size, size), jnp.int32)
    for k in range(1, parts):
        part = part + (col >= k * group).astype(jnp.int32)
    return jnp.where(out_row == parts * (col - group * part) + part, 1.0, 0.0).astype(BF)


def dot_f32(a, b):
    return jnp.dot(a, b, preferred_element_type=F32)


def third_to_out(k, start, size):
    at = lax.broadcasted_iota(jnp.int32, (1, size), 1) + start
    device, j = at // 32, at % 32
    target = jnp.where(j >= 24, 24 * device + 3 * (j - 24) + k, -1)
    out_row = lax.broadcasted_iota(jnp.int32, (192, size), 0)
    return jnp.where(out_row == target, 1.0, 0.0).astype(BF)


def feature_places():
    at = lax.broadcasted_iota(jnp.int32, (1, 1024), 1)
    r, device, j = (at % 512) // 128, 4 * (at // 512) + (at % 128) // 32, at % 32
    target = jnp.where(j < 24, 4 * (24 * device + j) + r, -1)
    feature = lax.broadcasted_iota(jnp.int32, (768, 1024), 0)
    return jnp.where(feature == target, 1.0, 0.0).astype(BF)


def dot_nt(a, b):
    return lax.dot_general(a, b, (((1,), (1,)), ((), ())), preferred_element_type=F32)


def dot_tn(a, b):
    return lax.dot_general(a, b, (((0,), (0,)), ((), ())), preferred_element_type=F32)


def unpack_small(packed, small):
    for t in range(4):
        small[t] = jnp.concatenate([packed[t, i : i + 1, :] for i in range(6)], axis=1)


def norm_vectors(small, norm):
    for i in range(6):
        at = 1152 + 192 * i
        norm[i : i + 1, :] = jnp.concatenate([small[t, 0:1, at : at + 192] for t in range(4)], axis=1)


def row_loop(body, step=128):
    @pl.loop(0, 512 // step)
    def _(i):
        body(pl.ds(pl.multiple_of(i * step, step), step))


def forward_kernel(
    master,
    owners,
    order_col,
    labels,
    flags,
    x_in,
    gy_in,
    w_att,
    w_up,
    w_down,
    w_qkv,
    w_out,
    slot_out,
    small_out,
    x_out,
    gy_row,
    qkv_out,
    prob_out,
    att_out,
    n_one_out,
    h_out,
    act_out,
    pull_out,
    z_two_out,
    inv_out,
    slot_row,
    slot_col,
    id_row,
    id_col,
    slots,
    canon_att,
    canon_ffn,
    land_att,
    land_ffn,
    pass_ffn,
    pass_land,
    share,
    p_att,
    p_up,
    p_down,
    small_mine,
    small_land,
    small_total,
    packed,
    small,
    norm,
    bias_qkv,
    v_att,
    v_qkv,
    v_compact,
    v_up,
    v_down,
    x_row,
    x_wide,
    qkv,
    prob,
    att,
    n_one,
    h_low,
    act,
    pull,
    total,
    inv,
    send_sems,
    recv_sems,
    local_sems,
):
    place = Place()
    link = Sender(send_sems, recv_sems, local_sems)
    place.hail()
    slots[place.c] = master[...].astype(BF)

    place.meet()
    whole = (w_att, w_up, w_down)
    held = (v_att, v_up, v_down)
    piece = (p_att, p_up, p_down)
    peers = (place.right, place.down, place.diag)
    mine_rows = pl.ds(pl.multiple_of(place.t * 128, 128), 128)
    tidy = []

    core_slots = link.send(slots.at[place.c], slots.at[place.c], place.core)
    x_moves = [
        link.send(x_in.at[place.ahead[k]], x_row.at[mine_rows], place.deep[k]) for k in (1, 2, 3)
    ]
    x_stay = link.copy(x_in.at[place.t], x_row.at[mine_rows])
    tidy.append(link.copy(gy_in.at[place.t], gy_row.at[mine_rows]))

    blocks = owners.shape[0]
    wide = slot_row.shape[1]
    owner = jnp.concatenate(
        [owners[...].astype(F32)[None], jnp.full((1, wide - blocks), -1.0, F32)], axis=1
    )
    kinds = lax.broadcasted_iota(jnp.int32, (8, wide), 0).astype(F32)
    owned = jnp.where(kinds == owner, 1.0, 0.0)
    ordinal = lax.broadcasted_iota(jnp.int32, (wide, wide), 1)
    earlier = jnp.where(lax.broadcasted_iota(jnp.int32, (wide, wide), 0) < ordinal, 1.0, 0.0)
    ahead = dot_f32(owned.astype(BF), earlier.astype(BF))
    ranking = jnp.sum(owned * ahead, axis=0, keepdims=True)
    place_of = jnp.where(order_col[...] == ordinal, 1.0, 0.0).astype(BF)
    pair = jnp.where(kinds == 0.0, owner, ranking).astype(BF)
    row = dot_nt(pair, place_of)
    col = dot_nt(place_of, pair)
    per_owner = float(master.shape[0])
    slot_row[...] = jnp.broadcast_to(row[0:1, :] * per_owner + row[1:2, :], slot_row.shape)
    slot_col[...] = jnp.broadcast_to(col[:, 0:1] * per_owner + col[:, 1:2], slot_col.shape)

    own = pl.ds(place.t, 1)
    apart = -1 - lax.broadcasted_iota(jnp.int32, (1, 512), 1)
    ids = jnp.where(flags[own, :] == 1, labels[own, :], apart).astype(F32)
    id_row[...] = jnp.broadcast_to(ids, id_row.shape)
    id_col[...] = jnp.transpose(id_row[...])
    tidy.append(link.copy(slot_row, slot_out))
    core_slots.wait_recv()

    pair_slots = slots[...].reshape(384, 2304)
    slot_id = (lax.broadcasted_iota(jnp.int32, (64, 384), 1) + place.xy * 384).astype(F32)
    order = [(3, place.diag), (1, place.right), (2, place.down), (0, None)]

    def spread(lo, rows, canon, land):
        sent = []
        for j, peer in order:
            at = place.xy if peer is None else peer[0] // 2
            spot = pl.ds(pl.multiple_of(place.c * 384 + at * 96 + lo, 32), rows)
            wanted = slot_col[spot, 0:1]
            pick = jnp.where(wanted == slot_id[:rows], 1.0, 0.0).astype(BF)
            canon[j] = dot_f32(pick, pair_slots).astype(BF)
            if peer is not None:
                sent.append(link.send(canon.at[j], land.at[j - 1], peer))
        return sent

    def collect(sent, lo, rows, canon, land):
        for move in sent:
            move.wait_recv()
        share[lo : lo + rows, :] = (
            canon[0].astype(F32) + land[0].astype(F32) + land[1].astype(F32) + land[2].astype(F32)
        )

    att_sent = spread(64, 32, canon_att, land_att)
    pick_small = jnp.where(slot_row[:, 768:769] == slot_id[:8], 1.0, 0.0).astype(BF)
    picked = dot_f32(pick_small, pair_slots)
    for i in range(6):
        small_mine[i : i + 1, :] = picked[0:1, 384 * i : 384 * i + 384]
    small_mine[6:8, :] = jnp.zeros((2, 384), F32)
    small_moves = [link.send(small_mine, small_land.at[j], peer) for j, peer in enumerate(peers)]
    def spread_halves():
        for j, peer in order:
            at = place.xy if peer is None else peer[0] // 2
            spot = pl.ds(pl.multiple_of(place.c * 384 + at * 96, 32), 64)
            pick = jnp.where(slot_col[spot, 0:1] == slot_id, 1.0, 0.0).astype(BF)
            canon_ffn[j] = dot_f32(pick, pair_slots).astype(BF)
            if j in (1, 3):
                half = canon_ffn.at[j, pl.ds(0, 32)]
                halves[j, 0] = link.send(half, land_ffn.at[0, j // 2], place.right)
            if j in (2, 3):
                half = canon_ffn.at[j, pl.ds(32, 32)]
                halves[j, 1] = link.send(half, land_ffn.at[1, j - 2], place.down)

    def pass_halves():
        halves[3, 0].wait_recv()
        pass_ffn[0] = canon_ffn[2, 0:32, :] + land_ffn[0, 1]
        halves["down"] = link.send(pass_ffn.at[0], pass_land.at[0], place.down)
        halves[3, 1].wait_recv()
        pass_ffn[1] = canon_ffn[1, 32:64, :] + land_ffn[1, 1]
        halves["right"] = link.send(pass_ffn.at[1], pass_land.at[1], place.right)

    def collect_halves():
        halves[1, 0].wait_recv()
        halves[2, 1].wait_recv()
        halves["down"].wait_recv()
        halves["right"].wait_recv()
        for i in range(2):
            share[32 * i : 32 * i + 32, :] = (
                canon_ffn[0, 32 * i : 32 * i + 32, :] + land_ffn[i, 0] + pass_land[i]
            ).astype(F32)

    halves = {}
    att_sent[0].wait_recv()
    spread_halves()
    collect(att_sent[1:], 64, 32, canon_att, land_att)

    for k in range(3):
        p_att[32 * k : 32 * k + 32, :] = share[64:96, 768 * k : 768 * k + 768].astype(BF)

    def spread_ffn():
        three = interleave(96, 3)
        for at, ref in ((0, p_up), (32, p_down)):
            parts = [share[at : at + 32, 768 * k : 768 * k + 768] for k in range(3)]
            ref[...] = dot_f32(three, jnp.concatenate(parts, axis=0).astype(BF)).astype(BF)

    deep_moves, right_moves, down_moves, own_copies, core_moves, loads = {}, {}, {}, {}, {}, {}

    def deep_send(w):
        spot = whole[w].at[place.t, rows_of(place, WEIGHTS[w][1])]
        own_copies[w] = link.copy(piece[w], spot)
        deep_moves[w] = [link.send(piece[w], spot, place.deep[k]) for k in (1, 2, 3)]

    def plane_send(w, k):
        rows = WEIGHTS[w][1]
        spot = whole[w].at[place.behind[k], rows_of(place, rows)]
        src = piece[w] if k == 0 else spot
        if k:
            deep_moves[w][k - 1].wait_recv()
        right_moves[w, k] = link.send(src, spot, place.right)
        down_moves[w, k] = link.send(src, spot, place.down)

    def plane_pass(w, k):
        rows = WEIGHTS[w][1]
        half = rows // 2
        right_moves[w, k].wait_recv()
        down_moves[w, k].wait_recv()
        t = place.behind[k]
        right_at = place.c * (4 * rows) + (place.right[0] // 2) * rows
        down_at = place.c * (4 * rows) + (place.down[0] // 2) * rows
        first = whole[w].at[t, pl.ds(pl.multiple_of(right_at, 16), half)]
        second = whole[w].at[t, pl.ds(pl.multiple_of(down_at + half, 16), half)]
        right_moves[w, k, 1] = link.send(second, second, place.right)
        down_moves[w, k, 1] = link.send(first, first, place.down)

    def core_pass(w, k):
        if k == 0:
            own_copies[w].wait()
        right_moves[w, k, 1].wait_recv()
        down_moves[w, k, 1].wait_recv()
        spot = whole[w].at[place.behind[k], half_of(place, WEIGHTS[w][1])]
        core_moves[w, k] = link.send(spot, spot, place.core)

    def load(w, k):
        core_moves[w, k].wait_recv()
        t = place.behind[k]
        loads[w, k] = link.copy(whole[w].at[t], held[w].at[t])

    def unpack(k):
        loads[0, k].wait()
        t = place.behind[k]
        thirds = [
            jnp.concatenate([v_att[t, 96 * d + 32 * k3 : 96 * d + 32 * k3 + 32, :] for d in range(8)], axis=0)
            for k3 in range(3)
        ]
        out = jnp.zeros((192, 768), F32)
        for k3 in range(3):
            out = out + dot_f32(third_to_out(k3, 0, 256), thirds[k3])
        v_compact[t] = out.astype(BF)
        turns = [
            thirds[0][:, :576],
            jnp.concatenate([thirds[0][:, 576:], thirds[1][:, :384]], axis=1),
            jnp.concatenate([thirds[1][:, 384:], thirds[2][:, :192]], axis=1),
            thirds[2][:, 192:],
        ]
        for half in range(2):
            for r in range(4):
                at = 512 * half + 128 * r
                v_qkv[t, at : at + 128, :] = turns[r][128 * half : 128 * half + 128]
        tidy.append(link.copy(v_qkv.at[t], w_qkv.at[t]))
        tidy.append(link.copy(v_compact.at[t], w_out.at[t]))

    def qkv_step(k):
        t = place.behind[k]

        def body(rows):
            lin = dot_f32(x_wide[rows, :], v_qkv[t]) + bias_qkv[t]
            qkv[t, rows, :] = lin.astype(BF)

        row_loop(body, 256)

    def attention(k):
        t = place.behind[k]

        def body(rows):
            allowed = id_col[rows, 0:1] == id_row[0:1, :]
            parts = []
            for i in range(3):
                at = 64 * i
                scores = dot_nt(qkv[t, rows, at : at + 64], qkv[t, :, 192 + at : 256 + at]) * 0.125
                scores = jnp.where(allowed, scores, MASKED)
                weight = jnp.exp(scores - jnp.max(scores, axis=1, keepdims=True))
                weight = weight * (1.0 / jnp.sum(weight, axis=1, keepdims=True))
                low = weight.astype(BF)
                prob[3 * t + i, rows, :] = low
                parts.append(dot_f32(low, qkv[t, :, 384 + at : 448 + at]))
            att[t, rows, :] = jnp.concatenate(parts, axis=1).astype(BF)

        row_loop(body, 256)
        tidy.append(link.copy(qkv.at[t], qkv_out.at[t]))
        tidy.append(link.copy(att.at[t], att_out.at[t]))
        tidy.append(link.copy(prob.at[pl.ds(3 * t, 3)], prob_out.at[pl.ds(3 * t, 3)]))

    def out_step():
        def body(rows):
            z = x_row[rows, :].astype(F32) + norm[0:1, :]
            for t in range(4):
                z = z + dot_f32(att[t, rows, :], v_compact[t])
            normed, inverse = normalize(z)
            n_one[rows, :] = normed
            inv[rows, :] = inverse
            h = normed * norm[2:3, :] + norm[3:4, :]
            h_low[rows, :] = h.astype(BF)
            total[rows, :] = h + norm[1:2, :]

        row_loop(body, 256)
        tidy.append(link.copy(n_one, n_one_out))
        tidy.append(link.copy(h_low, h_out))

    def up_step(k):
        loads[1, k].wait()
        t = place.behind[k]

        def body(rows):
            pre = dot_f32(h_low[rows, :], v_up[t]) + small[t, 0:1, 384:1152]
            below = 0.5 + 0.5 * lax.erf(pre * (0.5**0.5))
            act[t, rows, :] = (pre * below).astype(BF)
            slope = below + pre * (jnp.exp(-0.5 * pre * pre) * 0.3989422804014327)
            pull[t, rows, :] = slope.astype(BF)

        row_loop(body, 256)
        tidy.append(link.copy(act.at[t], act_out.at[t]))
        tidy.append(link.copy(pull.at[t], pull_out.at[t]))

    def down_step(k):
        loads[2, k].wait()
        t = place.behind[k]

        def body(rows):
            total[rows, :] += dot_f32(act[t, rows, :], v_down[t])

        row_loop(body, 256)

    def end_step():
        tidy.append(link.copy(total, z_two_out))
        tidy.append(link.copy(inv, inv_out))

    every = range(4)
    others = (1, 2, 3)
    small_state, gy_moves = {}, []

    def small_collect():
        for move in small_moves:
            move.wait_recv()
        small_total[...] = small_mine[...] + small_land[0] + small_land[1] + small_land[2]
        small_state["stay"] = link.copy(small_total, packed.at[place.t])
        small_state["deep"] = [
            link.send(small_total, packed.at[place.t], place.deep[k]) for k in others
        ]

    def small_ready():
        small_state["stay"].wait()
        for move in small_state["deep"]:
            move.wait_recv()
        unpack_small(packed, small)
        norm_vectors(small, norm)
        for t in every:
            bias_qkv[t] = jnp.concatenate(
                [small[t, 0:1, :192], jnp.zeros((1, 192), F32), small[t, 0:1, 192:384]], axis=1
            )
        tidy.append(link.copy(packed, small_out))

    def x_ready():
        x_stay.wait()
        for move in x_moves:
            move.wait_recv()
        places = feature_places()

        def body(rows):
            x_wide[rows, :] = dot_f32(x_row[rows, :], places).astype(BF)

        row_loop(body, 256)
        tidy.append(link.copy(x_wide, x_out))

    def gy_send():
        for k in others:
            gy_moves.append(link.send(gy_in.at[place.ahead[k]], gy_row.at[mine_rows], place.deep[k]))

    def gy_ready():
        for move in gy_moves:
            move.wait_recv()

    deep_send(0)
    small_collect()
    plane_send(0, 0)
    pass_halves()
    x_ready()
    plane_pass(0, 0)
    plane_send(0, 1)
    collect_halves()
    spread_ffn()
    deep_send(1)
    plane_send(2, 0)
    plane_send(0, 2)
    deep_send(2)
    core_pass(0, 0)
    plane_send(0, 3)
    plane_pass(0, 1)
    plane_pass(2, 0)
    load(0, 0)
    plane_pass(0, 3)
    unpack(0)
    plane_pass(0, 2)
    plane_send(1, 1)
    small_ready()
    qkv_step(0)
    attention(0)
    core_pass(0, 1)
    plane_send(1, 2)
    load(0, 1)
    core_pass(0, 2)
    plane_pass(1, 1)
    core_pass(0, 3)
    plane_send(1, 3)
    unpack(1)
    plane_send(2, 1)
    load(0, 2)
    qkv_step(1)
    load(0, 3)
    unpack(2)
    unpack(3)
    gy_send()
    core_pass(1, 1)
    core_pass(2, 0)
    plane_send(1, 0)
    qkv_step(3)
    attention(3)
    plane_pass(1, 3)
    qkv_step(2)
    load(1, 1)
    plane_pass(2, 1)
    attention(1)
    plane_pass(1, 0)
    plane_pass(1, 2)
    plane_send(2, 3)
    attention(2)
    core_pass(1, 3)
    core_pass(2, 1)
    out_step()
    load(2, 0)
    load(1, 3)
    core_pass(1, 0)
    plane_send(2, 2)
    up_step(1)
    load(2, 1)
    core_pass(1, 2)
    plane_pass(2, 3)
    up_step(3)
    load(1, 0)
    load(1, 2)
    plane_pass(2, 2)
    down_step(1)
    core_pass(2, 3)
    up_step(0)
    load(2, 3)
    gy_ready()
    core_pass(2, 2)
    up_step(2)
    load(2, 2)
    down_step(3)
    down_step(0)
    down_step(2)
    end_step()
    for copy in tidy:
        copy.wait()
    link.finish()


def forward_call(master, owners, order_col, labels, flags, x_in, gy_in):
    anywhere = pl.BlockSpec(memory_space=pl.ANY)
    vmem = pl.BlockSpec(memory_space=pltpu.VMEM)
    shape = jax.ShapeDtypeStruct
    outs = [
        ((4, 768, 768), BF),
        ((4, 768, 768), BF),
        ((4, 768, 768), BF),
        ((4, 1024, 576), BF),
        ((4, 192, 768), BF),
        ((8, 896), F32),
        ((4, 8, 384), F32),
        ((512, 1024), BF),
        ((512, 768), BF),
        ((4, 512, 576), BF),
        ((12, 512, 512), BF),
        ((4, 512, 192), BF),
        ((512, 768), F32),
        ((512, 768), BF),
        ((4, 512, 768), BF),
        ((4, 512, 768), BF),
        ((512, 768), F32),
        ((512, 1), F32),
    ]
    scratch = [
        ((8, 896), F32),
        ((896, 8), F32),
        ((8, 512), F32),
        ((512, 8), F32),
        ((2, 192, 2304), BF),
        ((4, 32, 2304), BF),
        ((4, 64, 2304), BF),
        ((3, 32, 2304), BF),
        ((2, 2, 32, 2304), BF),
        ((2, 32, 2304), BF),
        ((2, 32, 2304), BF),
        ((96, 2304), F32),
        ((96, 768), BF),
        ((96, 768), BF),
        ((96, 768), BF),
        ((8, 384), F32),
        ((3, 8, 384), F32),
        ((8, 384), F32),
        ((4, 8, 384), F32),
        ((4, 1, 2304), F32),
        ((8, 768), F32),
        ((4, 1, 576), F32),
        ((4, 768, 768), BF),
        ((4, 1024, 576), BF),
        ((4, 192, 768), BF),
        ((4, 768, 768), BF),
        ((4, 768, 768), BF),
        ((512, 768), BF),
        ((512, 1024), BF),
        ((4, 512, 576), BF),
        ((12, 512, 512), BF),
        ((4, 512, 192), BF),
        ((512, 768), F32),
        ((512, 768), BF),
        ((4, 512, 768), BF),
        ((4, 512, 768), BF),
        ((512, 768), F32),
        ((512, 1), F32),
    ]
    return pl.pallas_call(
        forward_kernel,
        out_shape=[shape(*o) for o in outs],
        in_specs=[vmem] * 5 + [anywhere] * 2,
        out_specs=[anywhere] * len(outs),
        scratch_shapes=[pltpu.VMEM(*s) for s in scratch]
        + [
            pltpu.SemaphoreType.DMA((128,)),
            pltpu.SemaphoreType.DMA((128,)),
            pltpu.SemaphoreType.DMA((64,)),
        ],
        compiler_params=pltpu.CompilerParams(
            collective_id=0, has_side_effects=True, vmem_limit_bytes=60 * MIB
        ),
        name="gather_and_forward",
    )(master, owners, order_col, labels, flags, x_in, gy_in)


def backward_kernel(
    labels,
    flags,
    gy_in,
    z_two_in,
    inv_in,
    small_in,
    act_in,
    pull_in,
    w_down,
    w_up,
    h_in,
    n_one_in,
    att_in,
    w_out,
    qkv_in,
    prob_in,
    w_qkv,
    x_in,
    blocks,
    small_out,
    out_mine,
    dx_mine,
    pool_out,
    *scratch,
):
    sums, cores, lefts, tops, lefts_two, tops_two, deeps = (scratch[3 * i : 3 * i + 3] for i in range(7))
    (
        ring,
        share,
        share_low,
        small_grad,
        small_land,
        packed,
        small,
        norm,
        gy,
        normed,
        inv,
        act,
        pull,
        v_down,
        v_up,
        h_low,
        att,
        v_out,
        qkv,
        prob,
        v_qkv,
        x_row,
        wide,
        low,
        total,
        d_up,
        d_att,
        d_qkv,
        turned,
        go,
        wide_sum,
        reds,
        red_up,
        red_qv,
        flag_col,
        row_low,
        pool,
        send_sems,
        recv_sems,
        local_sems,
    ) = scratch[21:]
    place = Place()
    place.hail()
    link = Sender(send_sems, recv_sems, local_sems)
    t_of = place.ahead
    steps = (1, 2, 3, 0)
    got = {}

    def fetch(name, src, dst):
        got[name] = link.copy(src, dst)

    fetch("small", small_in, packed)
    fetch("normed", z_two_in, normed)
    fetch("gy", gy_in, gy)
    fetch("inv", inv_in, inv)

    def load_ffn(i):
        t, slot = t_of[steps[i]], i % 2
        fetch(("act", i), act_in.at[t], act.at[slot])
        fetch(("down", i), w_down.at[t], v_down.at[slot])
        fetch(("pull", i), pull_in.at[t], pull.at[slot])
        fetch(("up", i), w_up.at[t], v_up.at[slot])

    def load_att(i):
        t, slot = t_of[steps[i]], i % 2
        fetch(("prob", i), prob_in.at[pl.ds(3 * t, 3)], prob.at[slot])
        fetch(("qkv", i), w_qkv.at[t], v_qkv.at[slot])

    own = pl.ds(place.t, 1)
    own_flags = flags[own, :].astype(F32)
    flag_col[...] = jnp.transpose(jnp.broadcast_to(own_flags, (8, 512)))
    t, x, y, c = place.t, place.x, place.y, place.c
    moves, stay = [], []

    core_moves, first, second, third = {}, {}, {}, {}
    ring_open = [None] * 3
    ring_at = [0]

    def chip_row(w, k, yy, xx, half):
        rows = WEIGHTS[w][1]
        at = pl.multiple_of((yy * 2 + xx) * rows + half * (rows // 2), 16)
        return sums[w].at[t_of[k], pl.ds(at, rows // 2)]

    def produce(w, k, make):
        slot = ring_at[0] % 3
        ring_at[0] += 1
        if ring_open[slot] is not None:
            link.sent(ring_open[slot])
        away = ring.at[slot]
        away[...] = make(1 - c).astype(BF)
        move = link.send(away, cores[w].at[k], place.core)
        ring_open[slot] = move
        core_moves[w, k] = move
        sums[w][t_of[k]] = make(c).astype(BF)

    def core_add(w, k):
        core_moves[w, k].wait_recv()
        rows = WEIGHTS[w][1]

        @pl.loop(0, 4)
        def _(i):
            at = pl.ds(pl.multiple_of(i * rows, 32), rows)
            sums[w][t_of[k], at, :] += cores[w][k, at, :]

        first[w, k] = []
        for i in (0, 1):
            first[w, k].append(link.send(chip_row(w, k, i, 1 - x, 0), lefts[w].at[k, i], place.right))
            first[w, k].append(link.send(chip_row(w, k, 1 - y, i, 1), tops[w].at[k, i], place.down))

    def add(spot, other):
        spot[...] = spot[...] + other[...]

    def plane_add(w, k):
        for move in first[w, k]:
            move.wait_recv()
        down_part, right_part = chip_row(w, k, 1 - y, x, 0), chip_row(w, k, y, 1 - x, 1)
        add(down_part, lefts[w].at[k, 1 - y])
        add(right_part, tops[w].at[k, 1 - x])
        second[w, k] = [
            link.send(down_part, lefts_two[w].at[k], place.down),
            link.send(right_part, tops_two[w].at[k], place.right),
        ]
        add(chip_row(w, k, y, x, 0), lefts[w].at[k, y])
        add(chip_row(w, k, y, x, 1), tops[w].at[k, x])

    def deep_add(w, k):
        for move in second[w, k]:
            move.wait_recv()
        add(chip_row(w, k, y, x, 0), lefts_two[w].at[k])
        add(chip_row(w, k, y, x, 1), tops_two[w].at[k])
        rows = WEIGHTS[w][1]
        if k:
            spot = pl.ds(pl.multiple_of(place.xy * rows, 16), rows)
            third[w, k] = link.send(sums[w].at[t_of[k], spot], deeps[w].at[k - 1], place.deep[k])

    def end(w):
        rows = WEIGHTS[w][1]
        spot = pl.ds(pl.multiple_of(place.xy * rows, 16), rows)
        whole = sums[w][t, spot, :].astype(F32)
        for k in (1, 2, 3):
            third[w, k].wait_recv()
            whole = whole + deeps[w][k - 1].astype(F32)
        whole = whole.astype(BF)
        if w == 0:
            for k in range(3):
                share[64:96, 768 * k : 768 * k + 768] = whole[32 * k : 32 * k + 32, :].astype(F32)
        else:
            at = 0 if w == 1 else 32
            parts = dot_tn(interleave(96, 3), whole)
            for k in range(3):
                share[at : at + 32, 768 * k : 768 * k + 768] = parts[32 * k : 32 * k + 32]

    def column_sum(value):
        return jnp.sum(value, axis=0, keepdims=True)

    def norm_two_back():
        def body(rows):
            grad = gy[rows, :].astype(F32) * flag_col[rows, 0:1]
            n, inverse = normalize(normed[rows, :])
            normed[rows, :] = n
            dz = norm_back(grad * norm[4:5, :], n, inverse)
            wide[rows, :] = dz
            total[rows, :] = dz
            low[rows, :] = dz.astype(BF)
            reds[4:5, :] += column_sum(grad * n)
            reds[5:6, :] += column_sum(grad)
            reds[1:2, :] += column_sum(dz)

        row_loop(body)

    def emit_out():
        sentence = lax.broadcasted_iota(jnp.int32, (SMAX, 512), 0).astype(F32)
        member = jnp.where((sentence == labels[own, :].astype(F32)) & (own_flags == 1.0), 1.0, 0.0)
        count = jnp.maximum(jnp.sum(member, axis=1, keepdims=True), 1.0)
        pooled = jnp.zeros((SMAX, 768), F32)
        for i in range(4):
            rows = slice(128 * i, 128 * i + 128)
            out = normed[rows, :] * norm[4:5, :] + norm[5:6, :]
            row_low[rows, :] = out.astype(BF)
            pooled = pooled + jnp.dot(
                member[:, rows], out, precision=exact_precision, preferred_element_type=F32
            )
        pool[...] = pooled / count
        own_rows = pl.ds(pl.multiple_of(t * 128, 128), 128)
        stay.append(link.copy(row_low.at[own_rows], out_mine.at[t]))
        stay.append(link.copy(pool, pool_out.at[t]))
        for k in (1, 2, 3):
            part = row_low.at[pl.ds(pl.multiple_of(t_of[k] * 128, 128), 128)]
            moves.append(link.send(part, out_mine.at[t], place.deep[k]))
            moves.append(link.send(pool, pool_out.at[t], place.deep[k]))

    def lanes(which):
        return pl.ds(pl.multiple_of(which * 384, 128), 384)

    def down_piece(i):
        k, slot = steps[i], i % 2
        got["act", i].wait()
        produce(2, k, lambda which: dot_tn(act[slot, :, lanes(which)], low[...]))

    def act_back(i):
        k, slot = steps[i], i % 2
        got["down", i].wait()
        got["pull", i].wait()

        def body(rows):
            grad = dot_nt(low[rows, :], v_down[slot]) * pull[slot, rows, :].astype(F32)
            red_up[t_of[k]] += column_sum(grad)
            d_up[rows, :] = grad.astype(BF)

        row_loop(body, 256)

    def up_piece(i):
        if i == 0:
            got["h"].wait()
        produce(1, steps[i], lambda which: dot_tn(h_low[:, lanes(which)], d_up[...]))

    def hidden_back(i):
        slot = i % 2
        got["up", i].wait()

        def body(rows):
            total[rows, :] += dot_nt(d_up[rows, :], v_up[slot])

        row_loop(body, 256)
        if i == 1:
            fetch("n_one", n_one_in, normed)

    def norm_one_back():
        got["n_one"].wait()

        def body(rows):
            dh = total[rows, :]
            n = normed[rows, :]
            dz = norm_back(dh * norm[2:3, :], n, inv[rows, :])
            total[rows, :] = dz
            low[rows, :] = dz.astype(BF)
            reds[2:3, :] += column_sum(dh * n)
            reds[3:4, :] += column_sum(dh)
            reds[0:1, :] += column_sum(dz)

        row_loop(body)

    def out_piece(i):
        k = steps[i]
        if i == 0:
            got["att"].wait()
            got["wout"].wait()
        go[...] = dot_tn(att[t_of[k]], low[...]).astype(BF)

        def body(rows):
            d_att[rows, :] = dot_nt(low[rows, :], v_out[t_of[k]]).astype(BF)

        row_loop(body, 256)

    def attention_back(i):
        k, slot = steps[i], i % 2
        tk = t_of[k]
        if i == 0:
            got["qkvs"].wait()
        got["prob", i].wait()
        turned[...] = jnp.zeros_like(turned)

        def body(rows):
            d_queries = []
            for j in range(3):
                at = 64 * j
                grad = d_att[rows, at : at + 64]
                weight_low = prob[slot, j, rows, :]
                weight = weight_low.astype(F32)
                d_prob = dot_nt(grad, qkv[tk, :, 384 + at : 448 + at]) * weight
                inner = jnp.sum(d_prob, axis=1, keepdims=True)
                d_scores = (d_prob - weight * inner).astype(BF)
                d_queries.append(dot_f32(d_scores, qkv[tk, :, 192 + at : 256 + at]))
                turned[at : at + 64, :] += dot_tn(qkv[tk, rows, at : at + 64], d_scores)
                turned[192 + at : 256 + at, :] += dot_tn(grad, weight_low)
            dq = jnp.concatenate(d_queries, axis=1) * 0.125
            red_qv[tk, :, :192] += column_sum(dq)
            d_qkv[rows, :192] = dq.astype(BF)

        row_loop(body, 256)
        dk = jnp.transpose(turned[:192, :]) * 0.125
        dv = jnp.transpose(turned[192:, :])
        red_qv[tk, :, 192:] += column_sum(dv)
        d_qkv[:, 192:] = jnp.concatenate([dk, dv], axis=1).astype(BF)

    def qkv_piece(i):
        k, slot = steps[i], i % 2
        if i == 0:
            got["x"].wait()

        def make(which):
            at = pl.ds(pl.multiple_of(512 * which, 512), 512)
            both = dot_tn(x_row[:, at], d_qkv[...])
            parts = [both[128 * r : 128 * r + 128] for r in range(4)]
            thirds = [
                jnp.concatenate([parts[0], parts[1][:, :192]], axis=1),
                jnp.concatenate([parts[1][:, 192:], parts[2][:, :384]], axis=1),
                jnp.concatenate([parts[2][:, 384:], parts[3]], axis=1),
            ]
            for k3 in range(3):
                thirds[k3] = thirds[k3] + dot_tn(third_to_out(k3, 128 * which, 128), go[...])
            return jnp.concatenate(
                [thirds[k3][32 * d : 32 * d + 32] for d in range(4) for k3 in range(3)], axis=0
            )

        produce(0, k, make)
        got["qkv", i].wait()

        def body(rows):
            wide_sum[rows, :] += dot_nt(d_qkv[rows, :], v_qkv[slot])

        row_loop(body, 256)

    sent, passed, across = {}, {}, {}

    def share_send(lo, hi):
        share_low[lo:hi, :] = share[lo:hi, :].astype(BF)
        mine = c * 4 + place.xy
        rows = pl.ds(lo, hi - lo)
        sent[lo] = (
            link.copy(share_low.at[rows], blocks.at[mine, rows]),
            link.send(share_low.at[rows], blocks.at[mine, rows], place.right),
            link.send(share_low.at[rows], blocks.at[mine, rows], place.down),
        )

    def share_pass(lo, hi):
        half = (hi - lo) // 2
        sent[lo][1].wait_recv()
        sent[lo][2].wait_recv()
        one = blocks.at[c * 4 + place.right[0] // 2, pl.ds(lo, half)]
        two = blocks.at[c * 4 + place.down[0] // 2, pl.ds(lo + half, half)]
        passed[lo] = link.send(one, one, place.down), link.send(two, two, place.right)

    def share_across(lo, hi):
        sent[lo][0].wait()
        passed[lo][0].wait_recv()
        passed[lo][1].wait_recv()
        spot = blocks.at[pl.ds(c * 4, 4), pl.ds(lo, hi - lo)]
        across[lo] = link.send(spot, spot, place.core)

    def share_ready(lo):
        across[lo].wait_recv()

    got["small"].wait()
    unpack_small(packed, small)
    norm_vectors(small, norm)
    reds[...] = jnp.zeros_like(reds)
    red_up[...] = jnp.zeros_like(red_up)
    red_qv[...] = jnp.zeros_like(red_qv)
    small_grad[...] = jnp.zeros_like(small_grad)
    wide_sum[...] = jnp.zeros_like(wide_sum)
    for name in ("normed", "gy", "inv"):
        got[name].wait()
    def load_rest():
        fetch("h", h_in, h_low)
        fetch("att", att_in, att)
        fetch("wout", w_out, v_out)
        fetch("qkvs", qkv_in, qkv)
        fetch("x", x_in, x_row)

    small_state = {}

    def meet():
        place.meet()

    def small_send():
        places = feature_places()

        def dx_body(rows):
            value = wide_sum[rows, :]
            high = value.astype(BF)
            rest = (value - high.astype(F32)).astype(BF)
            back = dot_nt(high, places) + dot_nt(rest, places)
            low[rows, :] = (total[rows, :] + back).astype(BF)

        row_loop(dx_body, 256)
        for q in range(4):
            at = slice(192 * q, 192 * q + 192)
            line = jnp.concatenate(
                [red_qv[q], red_up[q]] + [reds[i : i + 1, at] for i in range(6)], axis=1
            )
            for i in range(6):
                small_grad[q, i : i + 1, :] = line[:, 384 * i : 384 * i + 384]
        small_state["keep"] = link.copy(small_grad.at[t], small_land.at[6])
        small_state["deep"] = [
            link.send(small_grad.at[t_of[k]], small_land.at[k - 1], place.deep[k]) for k in (1, 2, 3)
        ]

    def dx_send():
        own_rows = pl.ds(pl.multiple_of(t * 128, 128), 128)
        stay.append(link.copy(low.at[own_rows], dx_mine.at[t]))
        for k in (1, 2, 3):
            part = low.at[pl.ds(pl.multiple_of(t_of[k] * 128, 128), 128)]
            moves.append(link.send(part, dx_mine.at[t], place.deep[k]))

    def small_core():
        small_state["keep"].wait()
        for move in small_state["deep"]:
            move.wait_recv()
        small_land[7] = small_land[6] + small_land[0] + small_land[1] + small_land[2]
        small_state["core"] = link.send(small_land.at[7], small_land.at[3], place.core)

    def small_right():
        small_state["core"].wait_recv()
        small_land[8] = small_land[7] + small_land[3]
        small_state["right"] = link.send(small_land.at[8], small_land.at[4], place.right)

    def small_down():
        small_state["right"].wait_recv()
        small_land[9] = small_land[8] + small_land[4]
        small_state["down"] = link.send(small_land.at[9], small_land.at[5], place.down)

    def small_end():
        small_state["down"].wait_recv()
        small_out[...] = small_land[9] + small_land[5]

    load_ffn(0)
    norm_two_back()
    meet()
    load_ffn(1)
    down_piece(0)
    load_rest()
    act_back(0)
    load_att(0)
    load_att(1)
    up_piece(0)
    hidden_back(0)
    core_add(2, 1)
    core_add(1, 1)
    load_ffn(2)
    emit_out()
    down_piece(1)
    act_back(1)
    plane_add(2, 1)
    core_add(2, 2)
    up_piece(1)
    hidden_back(1)
    load_ffn(3)
    core_add(1, 2)
    down_piece(2)
    act_back(2)
    up_piece(2)
    hidden_back(2)
    core_add(2, 3)
    plane_add(1, 1)
    plane_add(2, 2)
    deep_add(2, 1)
    down_piece(3)
    act_back(3)
    plane_add(1, 2)
    up_piece(3)
    hidden_back(3)
    norm_one_back()
    core_add(2, 0)
    core_add(1, 3)
    plane_add(2, 3)
    deep_add(1, 1)
    core_add(1, 0)
    out_piece(0)
    attention_back(0)
    deep_add(2, 2)
    deep_add(1, 2)
    qkv_piece(0)
    core_add(0, 1)
    load_att(2)
    out_piece(1)
    attention_back(1)
    qkv_piece(1)
    load_att(3)
    core_add(0, 2)
    out_piece(2)
    deep_add(2, 3)
    plane_add(1, 3)
    attention_back(2)
    qkv_piece(2)
    plane_add(0, 2)
    core_add(0, 3)
    plane_add(1, 0)
    deep_add(1, 3)
    out_piece(3)
    attention_back(3)
    deep_add(0, 2)
    plane_add(0, 1)
    qkv_piece(3)
    plane_add(0, 3)
    deep_add(1, 0)
    core_add(0, 0)
    small_send()
    plane_add(2, 0)
    deep_add(0, 1)
    end(1)
    deep_add(0, 3)
    small_core()
    plane_add(0, 0)
    deep_add(2, 0)
    end(2)
    share_send(0, 64)
    dx_send()
    small_right()
    deep_add(0, 0)
    end(0)
    share_send(64, 96)
    share_pass(0, 64)
    share_pass(64, 96)
    share_across(0, 64)
    small_down()
    share_across(64, 96)
    share_ready(64)
    small_end()
    share_ready(0)
    for move in moves:
        move.wait_recv()
    for copy in stay:
        copy.wait()
    link.finish()


def backward_call(*args):
    anywhere = pl.BlockSpec(memory_space=pl.ANY)
    vmem = pl.BlockSpec(memory_space=pltpu.VMEM)
    shape = jax.ShapeDtypeStruct
    sums = [((4, 4 * rows, cols), BF) for cols, rows in WEIGHTS]
    halves = [((4, 2, rows // 2, cols), BF) for cols, rows in WEIGHTS]
    singles = [((4, rows // 2, cols), BF) for cols, rows in WEIGHTS]
    deeps = [((3, rows, cols), BF) for cols, rows in WEIGHTS]
    rest = [
        ((3, 384, 768), BF),
        ((96, 2304), F32),
        ((96, 2304), BF),
        ((4, 8, 384), F32),
        ((11, 8, 384), F32),
        ((4, 8, 384), F32),
        ((4, 1, 2304), F32),
        ((8, 768), F32),
        ((512, 768), BF),
        ((512, 768), F32),
        ((512, 1), F32),
        ((2, 512, 768), BF),
        ((2, 512, 768), BF),
        ((2, 768, 768), BF),
        ((2, 768, 768), BF),
        ((512, 768), BF),
        ((4, 512, 192), BF),
        ((4, 192, 768), BF),
        ((4, 512, 576), BF),
        ((2, 3, 512, 512), BF),
        ((2, 1024, 576), BF),
        ((512, 1024), BF),
        ((512, 768), F32),
        ((512, 768), BF),
        ((512, 768), F32),
        ((512, 768), BF),
        ((512, 192), BF),
        ((512, 576), BF),
        ((384, 512), F32),
        ((192, 768), BF),
        ((512, 1024), F32),
        ((8, 768), F32),
        ((4, 1, 768), F32),
        ((4, 1, 384), F32),
        ((512, 8), F32),
        ((512, 768), BF),
        ((8, 768), F32),
    ]
    scratch = sums + sums + halves + halves + singles + singles + deeps + rest
    return pl.pallas_call(
        backward_kernel,
        out_shape=[
            shape((8, 96, 2304), BF),
            shape((8, 384), F32),
            shape((4, 128, 768), BF),
            shape((4, 128, 768), BF),
            shape((4, 8, 768), F32),
        ],
        in_specs=[vmem] * 2 + [anywhere] * 16,
        out_specs=[anywhere, vmem, anywhere, anywhere, anywhere],
        scratch_shapes=[pltpu.VMEM(*s) for s in scratch]
        + [
            pltpu.SemaphoreType.DMA((160,)),
            pltpu.SemaphoreType.DMA((160,)),
            pltpu.SemaphoreType.DMA((64,)),
        ],
        compiler_params=pltpu.CompilerParams(
            collective_id=1, has_side_effects=True, vmem_limit_bytes=62 * MIB
        ),
        name="backward_and_reduce",
    )(*args)


def finish_kernel(
    slot_row,
    blocks,
    small,
    pool,
    master,
    first,
    second,
    out_mine,
    dx_mine,
    new_master,
    new_first,
    new_second,
    layer_out,
    input_grad,
    pooled,
    norm_grads,
):
    step = pl.program_id(0)
    rows = master.shape[0]
    t = lax.axis_index("tensor")
    start = lax.axis_index("dp") * (rows * pl.num_programs(0)) + step * rows
    wanted = (lax.broadcasted_iota(jnp.int32, (rows, 1), 0) + start).astype(F32)
    match = slot_row[0:1, :768] == wanted
    gradient = dot_f32(jnp.where(match, 1.0, 0.0).astype(BF), blocks[...])
    is_small = slot_row[0:1, 768:769] == wanted
    small_line = jnp.concatenate([small[i : i + 1, :] for i in range(6)], axis=1)
    gradient = jnp.where(is_small, small_line, gradient)

    at = lax.broadcasted_iota(jnp.int32, (1, 768), 1) % 96
    rates = jnp.where(
        at < 32,
        MODEL_WIDTH ** (-0.5),
        jnp.where(
            at < 64,
            FF ** (-0.5),
            jnp.where(at < 88, MODEL_WIDTH ** (-0.5), 4.0 * MODEL_WIDTH ** (-0.5)),
        ),
    ).astype(F32)
    rate = jnp.sum(jnp.where(match, rates, 0.0), axis=1, keepdims=True)
    filled = (rate > 0.0) | is_small
    offset = lax.broadcasted_iota(jnp.int32, (1, small_line.shape[1]), 1) - 1152
    gain = ((offset >= 384) & (offset < 576)) | ((offset >= 768) & (offset < 960))
    small_rate = jnp.where(gain, 0.2, 0.1).astype(F32)
    step_rate = jnp.where(is_small, small_rate, rate)
    decay_on = jnp.where(is_small, 0.0, 1.0)
    new_master[...], new_first[...], new_second[...] = adamw(
        gradient, first[...], second[...], master[...], step_rate, decay_on, filled
    )
    for src, dst in ((out_mine, layer_out), (dx_mine, input_grad)):
        for row in range(4):
            dst[:, row, :] = src[row].astype(F32)

    @pl.when(step == 0)
    def _():
        total = jnp.zeros((4, 8, 192), F32)
        for q in range(4):
            total = total + jnp.where(t == q, pool[:, :, 192 * q : 192 * q + 192], 0.0)
        pooled[...] = total
        norm_grads[...] = jnp.concatenate(
            [small_line[:, 1152 + 192 * i : 1344 + 192 * i] for i in range(6)], axis=0
        )


def finish_call(slot_row, blocks, small, pool, master, first, second, out_mine, dx_mine):
    steps = 2
    slots, block_len = master.shape
    shape = jax.ShapeDtypeStruct

    def whole(*dims):
        return pl.BlockSpec(dims, lambda i: (0,) * len(dims))

    state = pl.BlockSpec((slots // steps, block_len), lambda i: (i, 0))
    token_in = pl.BlockSpec((4, 128 // steps, 768), lambda i: (0, i, 0))
    token_out = pl.BlockSpec((128 // steps, 4, 768), lambda i: (i, 0, 0))
    return pl.pallas_call(
        finish_kernel,
        grid=(steps,),
        out_shape=[shape((slots, block_len), F32)] * 3
        + [shape((128, 4, 768), F32)] * 2
        + [shape((4, 8, 192), F32), shape((6, 192), F32)],
        in_specs=[whole(8, 896), whole(768, block_len), whole(8, 384), whole(4, 8, 768)]
        + [state] * 3
        + [token_in] * 2,
        out_specs=[state] * 3 + [token_out] * 2 + [whole(4, 8, 192), whole(6, 192)],
        compiler_params=pltpu.CompilerParams(vmem_limit_bytes=62 * MIB),
        name="owners_update",
    )(slot_row, blocks, small, pool, master, first, second, out_mine, dx_mine)


def share_order():
    order = []
    for core in range(2):
        for chip in range(4):
            for base, count in ((0, 32), (256, 32), (512, 24), (704, 8)):
                at = base + (core * 4 + chip) * count
                order += list(range(at, at + count))
    return np.array(order + [768] + [4096] * 127, np.int32)


def local_rows(
    layer_input_rows,
    sentence_index_row,
    padding_mask,
    output_gradient,
    owner_rank,
    master_state,
    first_moment,
    second_moment,
):
    block_len = master_state.shape[2]
    order = share_order()
    (
        _,
        w_up,
        w_down,
        w_qkv,
        w_out,
        slot_row,
        small_all,
        x_row,
        gy_row,
        qkv,
        prob_low,
        attended,
        normed_one,
        h_low,
        act,
        pull,
        z_two,
        inverse,
    ) = forward_call(
        master_state[0],
        owner_rank,
        jnp.asarray(order[:, None]),
        sentence_index_row,
        padding_mask,
        jnp.transpose(layer_input_rows, (1, 0, 2)),
        jnp.transpose(output_gradient, (1, 0, 2)),
    )
    blocks, small_sum, out_mine, dx_mine, pool_all = backward_call(
        sentence_index_row,
        padding_mask,
        gy_row,
        z_two,
        inverse,
        small_all,
        act,
        pull,
        w_down,
        w_up,
        h_low,
        normed_one,
        attended,
        w_out,
        qkv,
        prob_low,
        w_qkv,
        x_row,
    )
    new_master, new_first, new_second, layer_out, input_grad, pooled, norm_grads = finish_call(
        slot_row,
        blocks.reshape(768, block_len),
        small_sum,
        pool_all,
        master_state[0],
        first_moment[0],
        second_moment[0],
        out_mine,
        dx_mine,
    )
    return (
        layer_out,
        pooled,
        input_grad,
        new_master[None],
        new_first[None],
        new_second[None],
        norm_grads,
    )


def solution(mesh):
    in_specs = (
        P("tensor", "dp", None),
        P("dp", None),
        P("dp", None),
        P("tensor", "dp", None),
        P(),
        P("tensor", "dp", None),
        P("tensor", "dp", None),
        P("tensor", "dp", None),
    )
    out_specs = (
        P("tensor", "dp", None),
        P("dp", None, "tensor"),
        P("tensor", "dp", None),
        P("tensor", "dp", None),
        P("tensor", "dp", None),
        P("tensor", "dp", None),
        P(None, "tensor"),
    )
    plain = mesh.shape["dp"] != 8 or mesh.shape["tensor"] != 4
    body = local_general if plain else local_rows
    return jax.shard_map(body, mesh=mesh, in_specs=in_specs, out_specs=out_specs, check_vma=False)
```

profile of v0, /device:TPU:9, one launch (start us, length us, event | category | flops | bytes accessed | tf_op | source)
XLA Modules:
  0.0 208.4 jit_solution(2404082254912187638)
XLA Ops:
  0.6 2.7 %copy_bitcast_fusion = (bf16[4,128,768]{2,1,0:T(8,128)(2,1)}, bf16[4,128,768]{2,1,0:T(8,128)(2,1)}) fusion(bf16[128,4,768]{2,1,0:T(4,128)(2,1)} %param.12, bf16[128,4,768]{2,1,0:T(4,128)(2,1)} %param.9), kind=kLoop, calls=%fused_computation | loop fusion | bytes 3145728 | tf_op jit(solution)/shard_map/transpose | solution.py:1793
  3.3 100.5 %gather_and_forward.1 = (bf16[4,768,768]{2,1,0:T(8,128)(2,1)}, bf16[4,768,768]{2,1,0:T(8,128)(2,1)}, bf16[4,768,768]{2,1,0:T(8,128)(2,1)}, bf16[4,1024,576]{2,1,...) custom-call(f32[192,2304]{1,0:T(8,128)} %bitcast.11, ...), custom_call_target="tpu_custom_call" | custom-call | tf_op jit(solution)/shard_map/gather_and_forward/pallas_call | solution.py:1020
  103.9 95.5 %backward_and_reduce.1 = (bf16[8,96,2304]{2,1,0:T(8,128)(2,1)}, f32[8,384]{1,0:T(8,128)}, bf16[4,128,768]{2,1,0:T(8,128)(2,1)}, bf16[4,128,768]{2,1,0:T(8,128)(2,1)}, f32[4,8,768]{2,1,0:T(8,128)}) custom-call(s32[4,512]{1,0:T(4,128)} %labels.3, s32[4,512]{1,0:T(4,128)} %flags.3, bf16[512,768]{1,0:T(8,128)(2,1)} %get-tuple-element.37.gy_in, ...), custom_call_target="tpu_custom_call" | custom-call | tf_op jit(solution)/shard_map/backward_and_reduce/pallas_call | solution.py:1631
  199.4 8.5 %owners_update.1 = (f32[192,2304]{1,0:T(8,128)}, f32[192,2304]{1,0:T(8,128)}, f32[192,2304]{1,0:T(8,128)}, f32[128,4,768]{2,1,0:T(4,128)}, f32[128,4,768]{2,1,0:...) custom-call(f32[8,896]{1,0:T(8,128)} %get-tuple-element.36.slot_row, bf16[768,2304]{1,0:T(8,128)(2,1)} %bitcast.13, ...), custom_call_target="tpu_custom_call" | custom-call | tf_op jit(solution)/shard_map/owners_update/pallas_call | solution.py:1730
where the time goes:
time: 212 us; the launch traced here: 208 us
  Pallas kernels  205 us (97%)
  local copies, waits for them, and re-layouts  2.71 us (1%)
    pallas_call x1, Pallas kernels, forward_call(): pl.pallas_call(forward_kernel, out_shape=[shape(*o) for o in outs], in_sp...  101 us
    pallas_call x1, Pallas kernels, backward_call(): pl.pallas_call(backward_kernel, out_shape=[shape((8, 96, 2304), BF), shap...  95.5 us
    pallas_call x1, Pallas kernels, finish_call(): pl.pallas_call(finish_kernel, grid=(steps,), out_shape=[shape((slots, blo...  8.5 us

commit v1 on v0

--- a/solution.py
+++ b/solution.py
@@ -871,82 +871,82 @@
     small_collect()
     plane_send(0, 0)
     pass_halves()
-    x_ready()
     plane_pass(0, 0)
     plane_send(0, 1)
     collect_halves()
     spread_ffn()
     deep_send(1)
-    plane_send(2, 0)
+    plane_send(1, 0)
     plane_send(0, 2)
-    deep_send(2)
+    plane_pass(0, 1)
+    small_ready()
     core_pass(0, 0)
     plane_send(0, 3)
-    plane_pass(0, 1)
-    plane_pass(2, 0)
+    x_ready()
+    core_pass(0, 1)
+    plane_pass(0, 2)
     load(0, 0)
+    plane_send(1, 1)
+    unpack(0)
+    load(0, 1)
     plane_pass(0, 3)
-    unpack(0)
-    plane_pass(0, 2)
-    plane_send(1, 1)
-    small_ready()
     qkv_step(0)
-    attention(0)
-    core_pass(0, 1)
+    plane_send(2, 0)
+    deep_send(2)
+    core_pass(0, 2)
+    unpack(1)
     plane_send(1, 2)
-    load(0, 1)
-    core_pass(0, 2)
-    plane_pass(1, 1)
+    load(0, 2)
+    qkv_step(1)
+    plane_pass(1, 0)
     core_pass(0, 3)
     plane_send(1, 3)
-    unpack(1)
+    attention(1)
+    gy_send()
+    unpack(2)
+    plane_pass(2, 0)
+    load(0, 3)
+    attention(0)
+    qkv_step(2)
+    plane_pass(1, 2)
+    core_pass(1, 0)
+    plane_pass(1, 1)
+    unpack(3)
+    attention(2)
+    plane_send(2, 2)
+    qkv_step(3)
+    plane_pass(1, 3)
+    load(1, 0)
+    plane_send(2, 3)
     plane_send(2, 1)
-    load(0, 2)
-    qkv_step(1)
-    load(0, 3)
-    unpack(2)
-    unpack(3)
-    gy_send()
+    core_pass(2, 0)
+    attention(3)
     core_pass(1, 1)
-    core_pass(2, 0)
-    plane_send(1, 0)
-    qkv_step(3)
-    attention(3)
-    plane_pass(1, 3)
-    qkv_step(2)
+    out_step()
     load(1, 1)
+    core_pass(1, 2)
+    load(2, 0)
+    core_pass(1, 3)
+    up_step(0)
+    plane_pass(2, 2)
+    load(1, 2)
+    load(1, 3)
+    plane_pass(2, 3)
+    up_step(1)
     plane_pass(2, 1)
-    attention(1)
-    plane_pass(1, 0)
-    plane_pass(1, 2)
-    plane_send(2, 3)
-    attention(2)
-    core_pass(1, 3)
+    up_step(2)
+    core_pass(2, 2)
+    gy_ready()
+    core_pass(2, 3)
+    up_step(3)
+    load(2, 2)
     core_pass(2, 1)
-    out_step()
-    load(2, 0)
-    load(1, 3)
-    core_pass(1, 0)
-    plane_send(2, 2)
-    up_step(1)
+    down_step(0)
+    load(2, 3)
+    down_step(2)
     load(2, 1)
-    core_pass(1, 2)
-    plane_pass(2, 3)
-    up_step(3)
-    load(1, 0)
-    load(1, 2)
-    plane_pass(2, 2)
+    down_step(3)
     down_step(1)
-    core_pass(2, 3)
-    up_step(0)
-    load(2, 3)
-    gy_ready()
-    core_pass(2, 2)
-    up_step(2)
-    load(2, 2)
-    down_step(3)
-    down_step(0)
-    down_step(2)
     end_step()
     for copy in tidy:
         copy.wait()
@@ -1487,86 +1487,86 @@
     load_rest()
     act_back(0)
     load_att(0)
+    core_add(2, 1)
     load_att(1)
     up_piece(0)
+    emit_out()
+    core_add(1, 1)
     hidden_back(0)
-    core_add(2, 1)
-    core_add(1, 1)
     load_ffn(2)
-    emit_out()
     down_piece(1)
+    plane_add(2, 1)
     act_back(1)
-    plane_add(2, 1)
     core_add(2, 2)
     up_piece(1)
     hidden_back(1)
     load_ffn(3)
+    plane_add(1, 1)
     core_add(1, 2)
     down_piece(2)
     act_back(2)
+    plane_add(2, 2)
+    core_add(2, 3)
+    deep_add(2, 1)
     up_piece(2)
+    deep_add(1, 1)
     hidden_back(2)
-    core_add(2, 3)
-    plane_add(1, 1)
-    plane_add(2, 2)
-    deep_add(2, 1)
     down_piece(3)
+    core_add(1, 3)
     act_back(3)
-    plane_add(1, 2)
     up_piece(3)
     hidden_back(3)
     norm_one_back()
+    out_piece(0)
+    plane_add(1, 2)
+    deep_add(2, 2)
+    core_add(1, 0)
+    attention_back(0)
+    plane_add(1, 3)
+    qkv_piece(0)
+    deep_add(1, 2)
+    plane_add(2, 3)
+    load_att(2)
+    core_add(0, 1)
     core_add(2, 0)
-    core_add(1, 3)
-    plane_add(2, 3)
-    deep_add(1, 1)
-    core_add(1, 0)
-    out_piece(0)
-    attention_back(0)
-    deep_add(2, 2)
-    deep_add(1, 2)
-    qkv_piece(0)
-    core_add(0, 1)
-    load_att(2)
     out_piece(1)
     attention_back(1)
+    deep_add(2, 3)
+    deep_add(1, 3)
     qkv_piece(1)
+    core_add(0, 2)
     load_att(3)
-    core_add(0, 2)
+    plane_add(0, 1)
     out_piece(2)
-    deep_add(2, 3)
-    plane_add(1, 3)
+    plane_add(1, 0)
     attention_back(2)
     qkv_piece(2)
     plane_add(0, 2)
     core_add(0, 3)
-    plane_add(1, 0)
-    deep_add(1, 3)
+    deep_add(0, 1)
     out_piece(3)
     attention_back(3)
+    plane_add(2, 0)
     deep_add(0, 2)
-    plane_add(0, 1)
     qkv_piece(3)
     plane_add(0, 3)
+    core_add(0, 0)
+    deep_add(2, 0)
+    small_send()
+    deep_add(0, 3)
+    end(2)
+    dx_send()
+    plane_add(0, 0)
     deep_add(1, 0)
-    core_add(0, 0)
-    small_send()
-    plane_add(2, 0)
-    deep_add(0, 1)
     end(1)
-    deep_add(0, 3)
-    small_core()
-    plane_add(0, 0)
-    deep_add(2, 0)
-    end(2)
     share_send(0, 64)
-    dx_send()
-    small_right()
     deep_add(0, 0)
     end(0)
     share_send(64, 96)
     share_pass(0, 64)
+    small_core()
     share_pass(64, 96)
+    small_right()
     share_across(0, 64)
     small_down()
     share_across(64, 96)

time: 212 us -> 208 us (0.981)
  the two profiles are of different devices: /device:TPU:9 before, /device:TPU:0 now
where the time goes in v1:
time: 208 us; the launch traced here: 204 us
  Pallas kernels  200 us (96%)
  local copies, waits for them, and re-layouts  2.71 us (1%)
    pallas_call x1, Pallas kernels, forward_call(): pl.pallas_call(forward_kernel, out_shape=[shape(*o) for o in outs], in_sp...  99 us
    pallas_call x1, Pallas kernels, backward_call(): pl.pallas_call(backward_kernel, out_shape=[shape((8, 96, 2304), BF), shap...  92.3 us
    pallas_call x1, Pallas kernels, finish_call(): pl.pallas_call(finish_kernel, grid=(steps,), out_shape=[shape((slots, blo...  8.5 us

profile of v1, /device:TPU:0, one launch (start us, length us, event | category | flops | bytes accessed | tf_op | source)
XLA Modules:
  0.0 203.7 jit_solution(10651926339246400836)
XLA Ops:
  0.6 2.7 %copy_bitcast_fusion = (bf16[4,128,768]{2,1,0:T(8,128)(2,1)}, bf16[4,128,768]{2,1,0:T(8,128)(2,1)}) fusion(bf16[128,4,768]{2,1,0:T(4,128)(2,1)} %param.12, bf16[128,4,768]{2,1,0:T(4,128)(2,1)} %param.9), kind=kLoop, calls=%fused_computation | loop fusion | bytes 3145728 | tf_op jit(solution)/shard_map/transpose | solution.py:1793
  3.3 99.0 %gather_and_forward.1 = (bf16[4,768,768]{2,1,0:T(8,128)(2,1)}, bf16[4,768,768]{2,1,0:T(8,128)(2,1)}, bf16[4,768,768]{2,1,0:T(8,128)(2,1)}, bf16[4,1024,576]{2,1,...) custom-call(f32[192,2304]{1,0:T(8,128)} %bitcast.11, ...), custom_call_target="tpu_custom_call" | custom-call | tf_op jit(solution)/shard_map/gather_and_forward/pallas_call | solution.py:1020
  102.4 92.3 %backward_and_reduce.1 = (bf16[8,96,2304]{2,1,0:T(8,128)(2,1)}, f32[8,384]{1,0:T(8,128)}, bf16[4,128,768]{2,1,0:T(8,128)(2,1)}, bf16[4,128,768]{2,1,0:T(8,128)(2,1)}, f32[4,8,768]{2,1,0:T(8,128)}) custom-call(s32[4,512]{1,0:T(4,128)} %labels.3, s32[4,512]{1,0:T(4,128)} %flags.3, bf16[512,768]{1,0:T(8,128)(2,1)} %get-tuple-element.37.gy_in, ...), custom_call_target="tpu_custom_call" | custom-call | tf_op jit(solution)/shard_map/backward_and_reduce/pallas_call | solution.py:1631
  194.7 8.5 %owners_update.1 = (f32[192,2304]{1,0:T(8,128)}, f32[192,2304]{1,0:T(8,128)}, f32[192,2304]{1,0:T(8,128)}, f32[128,4,768]{2,1,0:T(4,128)}, f32[128,4,768]{2,1,0:...) custom-call(f32[8,896]{1,0:T(8,128)} %get-tuple-element.36.slot_row, bf16[768,2304]{1,0:T(8,128)(2,1)} %bitcast.13, ...), custom_call_target="tpu_custom_call" | custom-call | tf_op jit(solution)/shard_map/owners_update/pallas_call | solution.py:1730
